TPU v7x, 32 devices: a whole 2x2x4 slice. The times are simulated.
32 devices in a mesh: row: 8 (over z, y), col: 4 (over x, core).
Axes of the slice: x: 2, y: 2, z: 4, core: 2. Of those that a mesh axis runs over, the one named last changes fastest.
Arguments:
- struct_disp: float32 [48, 8192], P(None, ('row', 'col')), may hold values from -6 to 6
- target: int32 [8192], P(('row', 'col')), may hold values from 0 to 32767, as said below
- inverse: bfloat16 [32768, 32768], P('row', 'col'), may hold values from -0.09375 to 0.09375
- centre_xyz: float32 [3, 32768], replicated, may hold values from 0 to 1, as said below
- node_xyz: float32 [3, 65536], P(None, ('row', 'col')), may hold values from 0 to 1, as said below
Outputs:
- volume_disp: float32 [48, 65536], P(None, ('row', 'col'))
Inputs may be any that keep to these rules, and one draw needn't show every extreme that they name: `target`: centre j is held by the owner of index r * 4 + c with c = j // 8192 and r = (j % 8192) // 1024. The 256 entries of one device name centres of at most 16 entries for any one owner, and one owner receives exactly 16 entries from every device. `centre_xyz`: every centre lies on the boundary of the cube that spans 0.3 to 0.7 in each coordinate. `node_xyz`: every volume node lies outside the cube that spans 0.3 to 0.7 in each coordinate, or on its boundary.
All inputs are finite; a program needn't handle non-finite values.
Results may differ from a plain program's by a relative error of at most 0.0049.
Values may be sent and summed in bfloat16 or wider, within the bound.
A program may use at most 128 MiB of HBM per device.

v0:
```python
import math

import jax
import jax.numpy as jnp
from jax import lax
from jax.sharding import PartitionSpec as P

M = 32768


def wendland_tile(centre_block, node_block):
    radius = 2.0 / math.sqrt(M)
    squared = jnp.zeros((centre_block.shape[1], node_block.shape[1]), jnp.float32)
    for component in range(3):
        difference = centre_block[component][:, None] - node_block[component][None, :]
        squared = squared + difference * difference
    scaled = jnp.sqrt(squared) / radius
    remain = jnp.maximum(1.0 - scaled, 0.0)
    return (remain**4 * (4.0 * scaled + 1.0)).astype(jnp.bfloat16)


def per_device(struct_disp, target, inverse, centre_xyz, node_xyz):
    row_count = lax.axis_size("row")
    col_count = lax.axis_size("col")
    owner_count = row_count * col_count
    row_block = inverse.shape[0]
    col_block = inverse.shape[1]
    owner_block = row_block // col_count
    disp_rows = struct_disp.shape[0]
    slot_cap = max(2, 2 * struct_disp.shape[1] // owner_count)
    owner_col = target // col_block
    owner_row = target % col_block // owner_block
    owner_ids = owner_row * col_count + owner_col
    offsets = target % owner_block
    one_hot = (owner_ids[:, None] == jnp.arange(owner_count, dtype=jnp.int32)[None, :]).astype(
        jnp.int32
    )
    ranking = jnp.sum(jnp.cumsum(one_hot, axis=0) * one_hot, axis=1) - 1
    slot_ids = owner_ids * slot_cap + ranking
    send_values = (
        jnp.zeros((owner_count * slot_cap, disp_rows), jnp.float32).at[slot_ids].set(struct_disp.T)
    )
    send_offsets = jnp.full((owner_count * slot_cap,), -1, jnp.int32).at[slot_ids].set(offsets)
    recv_values, recv_offsets = (
        lax.all_to_all(send_values, ("row", "col"), split_axis=0, concat_axis=0, tiled=True),
        lax.all_to_all(send_offsets, ("row", "col"), split_axis=0, concat_axis=0, tiled=True),
    )
    dest_rows = jnp.where(recv_offsets < 0, owner_block, recv_offsets).astype(jnp.int32)
    gathered_rows = (
        jnp.zeros((owner_block + 1, disp_rows), jnp.float32).at[dest_rows].add(recv_values)
    )
    centre_disp = gathered_rows[:owner_block].T
    disp_bf = centre_disp.astype(jnp.bfloat16)
    partial_value = lax.dot_general(
        lax.all_gather(disp_bf, "row", axis=1, tiled=True),
        inverse,
        (((1,), (1,)), ((), ())),
        preferred_element_type=jnp.float32,
    )
    zeros_init = jnp.zeros((disp_rows, node_xyz.shape[1]), jnp.float32)
    summed = lax.psum(partial_value, "col")
    coef_bf = summed.astype(jnp.bfloat16)
    shard_piece = lax.all_gather(coef_bf, "row", axis=1, tiled=True)
    piece_width = shard_piece.shape[1]
    block_size = math.gcd(piece_width, 2048)

    def one_block(counter, running_in):
        first_col = counter * block_size
        coef_part = lax.dynamic_slice_in_dim(shard_piece, first_col, block_size, 1)
        centres = lax.dynamic_slice_in_dim(centre_xyz, first_col, block_size, 1)
        kernel_tile = wendland_tile(centres, node_xyz)
        return running_in + jnp.dot(coef_part, kernel_tile, preferred_element_type=jnp.float32)

    return lax.fori_loop(0, piece_width // block_size, one_block, zeros_init)


def solution(mesh):
    placed = (
        P(None, ("row", "col")),
        P(("row", "col")),
        P("row", "col"),
        P(),
        P(None, ("row", "col")),
    )
    return jax.shard_map(
        per_device, mesh=mesh, in_specs=placed, out_specs=P(None, ("row", "col")), check_vma=False
    )
```

profile of v0, /device:TPU:13, one launch (start us, length us, event | category | flops | bytes accessed | tf_op | source)
XLA Modules:
  0.0 422.1 jit_solution(15410246992138416484)
XLA Ops:
  6.5 0.7 and_select_fusion
  7.2 0.6 reduce-window.6
  7.8 0.2 slice_reduce_fusion
  8.1 0.1 fusion.14
  8.2 1.4 scatter_custom_fusion
  9.6 0.7 all_to_all.16
  10.3 6.3 %all-to-all-start = ((s32[32,16,1]{1,2,0:T(1,128)}), s32[32,16,1]{1,2,0:T(1,128)S(1)}, u32[]{:S(2)}, u32[]{:S(2)}) async-start(s32[32,16,1]{1,2,0:T(1,128)} %bitcast.2), calls=%async_computation | async-start | bytes 32768 | tf_op jit(solution)/shard_map/all_to_all | solution.py:46
  16.6 0.9 copy.18
  17.5 1.2 scatter_custom_fusion.1
  18.7 0.9 reshape.94
  19.6 1.7 all-to-all-done
  21.3 5.0 %all-to-all-start.1 = ((f32[32,1,768]{2,1,0:T(1,128)}), f32[32,1,768]{2,1,0:T(1,128)S(1)}, u32[]{:S(2)}, u32[]{:S(2)}) async-start(f32[32,1,768]{2,1,0:T(1,128)} %reshape.94), calls=%async_computation.1 | async-start | bytes 196608 | tf_op jit(solution)/shard_map/all_to_all | solution.py:45
  26.2 0.0 all-gather.2.cloned.1.call-start
  26.3 0.6 broadcast.152
  26.9 0.7 reduce.5
  27.6 0.1 all_to_all.18
  27.7 4.3 %all-to-all-done.1 = f32[32,1,768]{2,1,0:T(1,128)S(1)} async-done(((f32[32,1,768]{2,1,0:T(1,128)}), f32[32,1,768]{2,1,0:T(1,128)S(1)}, u32[]{:S(2)}, u32[]{:S(2)}) %all-to-all-start.1) | async-done | bytes 98336 | tf_op jit(solution)/shard_map/all_to_all | solution.py:45
  32.0 0.5 broadcast.154
  32.5 0.9 reduce.6
  33.4 0.1 reshape.95
  33.5 2.9 scatter_custom_fusion.2
  36.5 0.1 copy.19
  36.6 22.3 %all_gather.6 = bf16[48,8192]{1,0:T(8,128)(2,1)S(1)} all-gather(bf16[48,1024]{1,0:T(8,128)(2,1)S(1)} %copy.19), channel_id=1, replica_groups=mesh['row'=8,'col'=4] {'row'}, dimensions={1}, use_global_device_ids=true | all-gather | bytes 884736 | tf_op jit(solution)/shard_map/all_gather | solution.py:55
  58.9 0.0 copy-start
  58.9 26.7 %fusion.20 = f32[48,4096]{1,0:T(8,128)S(1)} fusion(bf16[48,8192]{1,0:T(8,128)(2,1)S(1)} %all_gather.6, bf16[4096,8192]{1,0:T(8,128)(2,1)} %param.9), kind=kOutput, calls=%fused_computation.45 | convolution fusion | flops 3221225472 | bytes 68681728 | tf_op jit(solution)/shard_map/dot_general | solution.py:54
  85.6 25.0 %all-reduce.1 = bf16[48,4096]{1,0:T(8,128)(2,1)} all-reduce(f32[48,4096]{1,0:T(8,128)S(1)} %fusion.20), channel_id=1, replica_groups=mesh['row'=8,'col'=4] {'col'}, use_global_device_ids=true, to_apply=%region_6.7 | all-reduce | flops 196608 | bytes 1179648 | tf_op jit(solution)/shard_map/psum | solution.py:61
  110.6 0.0 all-gather.2.cloned.1.call-update
  110.6 61.3 %all-gather.2.cloned.1.call-done = bf16[48,32768]{1,0:T(8,128)(2,1)} async-done(((bf16[48,4096]{1,0:T(8,128)(2,1)}), bf16[48,32768]{1,0:T(8,128)(2,1)}) %all-gather.2.cloned.1.call-update) | async-done | bytes 3145744 | tf_op jit(solution)/shard_map/all_gather | solution.py:63
  171.9 0.0 copy-done
  171.9 242.6 %while.16 = (s32[]{:T(128)}, f32[48,2048]{1,0:T(8,128)S(1)}, bf16[48,32768]{1,0:T(8,128)(2,1)}, f32[3,32768]{1,0:T(4,128)}, f32[3,2048]{1,0:T(4,128)S(1)}, /*ind...) while((s32[]{:T(128)}, f32[48,2048]{1,0:T(8,128)S(1)}, ...), condition=%wide.region_8.9_spmd.clone, body=%wide.region_7.8_spmd.clone.sunk | while | flops 474152960 | bytes 1130701 | solution.py:74
  171.9 1.0 constant_dynamic-slice_fusion.2
  172.9 14.2 %fusion.26 = f32[48,2048]{1,0:T(8,128)S(1)} fusion(f32[2048]{0:T(1024)S(1)} %bitcast.50, f32[2048]{0:T(1024)S(1)} %bitcast.48, f32[2048]{0:T(1024)S(1)} %bitcast.49, f32[2048]{0:T(1024)S(1)} %bitcast.47, f32[2048]{0:T(1024)S(1)} %bitcast.51, f32[2048]{0:T(1024)S(1)} %bitcast.46, f32[48,2048]{1,0:T(8,128)S(1)} %get-tuple-element.232, ...), kind=kOutput, calls=%fused_computation.5.clone.1 | convolution fusion | flops 474152960 | bytes 1032197 | tf_op jit(solution)/shard_map/while/body/eval_jaxpr/dot_general | solution.py:72
  187.1 1.0 constant_dynamic-slice_fusion.2
  188.1 14.2 %fusion.26 = f32[48,2048]{1,0:T(8,128)S(1)} fusion(f32[2048]{0:T(1024)S(1)} %bitcast.50, f32[2048]{0:T(1024)S(1)} %bitcast.48, f32[2048]{0:T(1024)S(1)} %bitcast.49, f32[2048]{0:T(1024)S(1)} %bitcast.47, f32[2048]{0:T(1024)S(1)} %bitcast.51, f32[2048]{0:T(1024)S(1)} %bitcast.46, f32[48,2048]{1,0:T(8,128)S(1)} %get-tuple-element.232, ...), kind=kOutput, calls=%fused_computation.5.clone.1 | convolution fusion | flops 474152960 | bytes 1032197 | tf_op jit(solution)/shard_map/while/body/eval_jaxpr/dot_general | solution.py:72
  202.2 1.0 constant_dynamic-slice_fusion.2
  203.2 14.2 %fusion.26 = f32[48,2048]{1,0:T(8,128)S(1)} fusion(f32[2048]{0:T(1024)S(1)} %bitcast.50, f32[2048]{0:T(1024)S(1)} %bitcast.48, f32[2048]{0:T(1024)S(1)} %bitcast.49, f32[2048]{0:T(1024)S(1)} %bitcast.47, f32[2048]{0:T(1024)S(1)} %bitcast.51, f32[2048]{0:T(1024)S(1)} %bitcast.46, f32[48,2048]{1,0:T(8,128)S(1)} %get-tuple-element.232, ...), kind=kOutput, calls=%fused_computation.5.clone.1 | convolution fusion | flops 474152960 | bytes 1032197 | tf_op jit(solution)/shard_map/while/body/eval_jaxpr/dot_general | solution.py:72
  217.4 1.0 constant_dynamic-slice_fusion.2
  218.4 14.2 %fusion.26 = f32[48,2048]{1,0:T(8,128)S(1)} fusion(f32[2048]{0:T(1024)S(1)} %bitcast.50, f32[2048]{0:T(1024)S(1)} %bitcast.48, f32[2048]{0:T(1024)S(1)} %bitcast.49, f32[2048]{0:T(1024)S(1)} %bitcast.47, f32[2048]{0:T(1024)S(1)} %bitcast.51, f32[2048]{0:T(1024)S(1)} %bitcast.46, f32[48,2048]{1,0:T(8,128)S(1)} %get-tuple-element.232, ...), kind=kOutput, calls=%fused_computation.5.clone.1 | convolution fusion | flops 474152960 | bytes 1032197 | tf_op jit(solution)/shard_map/while/body/eval_jaxpr/dot_general | solution.py:72
  232.6 1.0 constant_dynamic-slice_fusion.2
  233.6 14.2 %fusion.26 = f32[48,2048]{1,0:T(8,128)S(1)} fusion(f32[2048]{0:T(1024)S(1)} %bitcast.50, f32[2048]{0:T(1024)S(1)} %bitcast.48, f32[2048]{0:T(1024)S(1)} %bitcast.49, f32[2048]{0:T(1024)S(1)} %bitcast.47, f32[2048]{0:T(1024)S(1)} %bitcast.51, f32[2048]{0:T(1024)S(1)} %bitcast.46, f32[48,2048]{1,0:T(8,128)S(1)} %get-tuple-element.232, ...), kind=kOutput, calls=%fused_computation.5.clone.1 | convolution fusion | flops 474152960 | bytes 1032197 | tf_op jit(solution)/shard_map/while/body/eval_jaxpr/dot_general | solution.py:72
  247.7 1.0 constant_dynamic-slice_fusion.2
  248.7 14.2 %fusion.26 = f32[48,2048]{1,0:T(8,128)S(1)} fusion(f32[2048]{0:T(1024)S(1)} %bitcast.50, f32[2048]{0:T(1024)S(1)} %bitcast.48, f32[2048]{0:T(1024)S(1)} %bitcast.49, f32[2048]{0:T(1024)S(1)} %bitcast.47, f32[2048]{0:T(1024)S(1)} %bitcast.51, f32[2048]{0:T(1024)S(1)} %bitcast.46, f32[48,2048]{1,0:T(8,128)S(1)} %get-tuple-element.232, ...), kind=kOutput, calls=%fused_computation.5.clone.1 | convolution fusion | flops 474152960 | bytes 1032197 | tf_op jit(solution)/shard_map/while/body/eval_jaxpr/dot_general | solution.py:72
  262.9 1.0 constant_dynamic-slice_fusion.2
  263.9 14.2 %fusion.26 = f32[48,2048]{1,0:T(8,128)S(1)} fusion(f32[2048]{0:T(1024)S(1)} %bitcast.50, f32[2048]{0:T(1024)S(1)} %bitcast.48, f32[2048]{0:T(1024)S(1)} %bitcast.49, f32[2048]{0:T(1024)S(1)} %bitcast.47, f32[2048]{0:T(1024)S(1)} %bitcast.51, f32[2048]{0:T(1024)S(1)} %bitcast.46, f32[48,2048]{1,0:T(8,128)S(1)} %get-tuple-element.232, ...), kind=kOutput, calls=%fused_computation.5.clone.1 | convolution fusion | flops 474152960 | bytes 1032197 | tf_op jit(solution)/shard_map/while/body/eval_jaxpr/dot_general | solution.py:72
  278.1 1.0 constant_dynamic-slice_fusion.2
  279.1 14.2 %fusion.26 = f32[48,2048]{1,0:T(8,128)S(1)} fusion(f32[2048]{0:T(1024)S(1)} %bitcast.50, f32[2048]{0:T(1024)S(1)} %bitcast.48, f32[2048]{0:T(1024)S(1)} %bitcast.49, f32[2048]{0:T(1024)S(1)} %bitcast.47, f32[2048]{0:T(1024)S(1)} %bitcast.51, f32[2048]{0:T(1024)S(1)} %bitcast.46, f32[48,2048]{1,0:T(8,128)S(1)} %get-tuple-element.232, ...), kind=kOutput, calls=%fused_computation.5.clone.1 | convolution fusion | flops 474152960 | bytes 1032197 | tf_op jit(solution)/shard_map/while/body/eval_jaxpr/dot_general | solution.py:72
  293.2 1.0 constant_dynamic-slice_fusion.2
  294.2 14.2 %fusion.26 = f32[48,2048]{1,0:T(8,128)S(1)} fusion(f32[2048]{0:T(1024)S(1)} %bitcast.50, f32[2048]{0:T(1024)S(1)} %bitcast.48, f32[2048]{0:T(1024)S(1)} %bitcast.49, f32[2048]{0:T(1024)S(1)} %bitcast.47, f32[2048]{0:T(1024)S(1)} %bitcast.51, f32[2048]{0:T(1024)S(1)} %bitcast.46, f32[48,2048]{1,0:T(8,128)S(1)} %get-tuple-element.232, ...), kind=kOutput, calls=%fused_computation.5.clone.1 | convolution fusion | flops 474152960 | bytes 1032197 | tf_op jit(solution)/shard_map/while/body/eval_jaxpr/dot_general | solution.py:72
  308.4 1.0 constant_dynamic-slice_fusion.2
  309.4 14.2 %fusion.26 = f32[48,2048]{1,0:T(8,128)S(1)} fusion(f32[2048]{0:T(1024)S(1)} %bitcast.50, f32[2048]{0:T(1024)S(1)} %bitcast.48, f32[2048]{0:T(1024)S(1)} %bitcast.49, f32[2048]{0:T(1024)S(1)} %bitcast.47, f32[2048]{0:T(1024)S(1)} %bitcast.51, f32[2048]{0:T(1024)S(1)} %bitcast.46, f32[48,2048]{1,0:T(8,128)S(1)} %get-tuple-element.232, ...), kind=kOutput, calls=%fused_computation.5.clone.1 | convolution fusion | flops 474152960 | bytes 1032197 | tf_op jit(solution)/shard_map/while/body/eval_jaxpr/dot_general | solution.py:72
  323.6 1.0 constant_dynamic-slice_fusion.2
  324.5 14.2 %fusion.26 = f32[48,2048]{1,0:T(8,128)S(1)} fusion(f32[2048]{0:T(1024)S(1)} %bitcast.50, f32[2048]{0:T(1024)S(1)} %bitcast.48, f32[2048]{0:T(1024)S(1)} %bitcast.49, f32[2048]{0:T(1024)S(1)} %bitcast.47, f32[2048]{0:T(1024)S(1)} %bitcast.51, f32[2048]{0:T(1024)S(1)} %bitcast.46, f32[48,2048]{1,0:T(8,128)S(1)} %get-tuple-element.232, ...), kind=kOutput, calls=%fused_computation.5.clone.1 | convolution fusion | flops 474152960 | bytes 1032197 | tf_op jit(solution)/shard_map/while/body/eval_jaxpr/dot_general | solution.py:72
  338.7 1.0 constant_dynamic-slice_fusion.2
  339.7 14.2 %fusion.26 = f32[48,2048]{1,0:T(8,128)S(1)} fusion(f32[2048]{0:T(1024)S(1)} %bitcast.50, f32[2048]{0:T(1024)S(1)} %bitcast.48, f32[2048]{0:T(1024)S(1)} %bitcast.49, f32[2048]{0:T(1024)S(1)} %bitcast.47, f32[2048]{0:T(1024)S(1)} %bitcast.51, f32[2048]{0:T(1024)S(1)} %bitcast.46, f32[48,2048]{1,0:T(8,128)S(1)} %get-tuple-element.232, ...), kind=kOutput, calls=%fused_computation.5.clone.1 | convolution fusion | flops 474152960 | bytes 1032197 | tf_op jit(solution)/shard_map/while/body/eval_jaxpr/dot_general | solution.py:72
  353.9 1.0 constant_dynamic-slice_fusion.2
  354.9 14.2 %fusion.26 = f32[48,2048]{1,0:T(8,128)S(1)} fusion(f32[2048]{0:T(1024)S(1)} %bitcast.50, f32[2048]{0:T(1024)S(1)} %bitcast.48, f32[2048]{0:T(1024)S(1)} %bitcast.49, f32[2048]{0:T(1024)S(1)} %bitcast.47, f32[2048]{0:T(1024)S(1)} %bitcast.51, f32[2048]{0:T(1024)S(1)} %bitcast.46, f32[48,2048]{1,0:T(8,128)S(1)} %get-tuple-element.232, ...), kind=kOutput, calls=%fused_computation.5.clone.1 | convolution fusion | flops 474152960 | bytes 1032197 | tf_op jit(solution)/shard_map/while/body/eval_jaxpr/dot_general | solution.py:72
  369.1 1.0 constant_dynamic-slice_fusion.2
  370.0 14.2 %fusion.26 = f32[48,2048]{1,0:T(8,128)S(1)} fusion(f32[2048]{0:T(1024)S(1)} %bitcast.50, f32[2048]{0:T(1024)S(1)} %bitcast.48, f32[2048]{0:T(1024)S(1)} %bitcast.49, f32[2048]{0:T(1024)S(1)} %bitcast.47, f32[2048]{0:T(1024)S(1)} %bitcast.51, f32[2048]{0:T(1024)S(1)} %bitcast.46, f32[48,2048]{1,0:T(8,128)S(1)} %get-tuple-element.232, ...), kind=kOutput, calls=%fused_computation.5.clone.1 | convolution fusion | flops 474152960 | bytes 1032197 | tf_op jit(solution)/shard_map/while/body/eval_jaxpr/dot_general | solution.py:72
  384.2 1.0 constant_dynamic-slice_fusion.2
  385.2 14.2 %fusion.26 = f32[48,2048]{1,0:T(8,128)S(1)} fusion(f32[2048]{0:T(1024)S(1)} %bitcast.50, f32[2048]{0:T(1024)S(1)} %bitcast.48, f32[2048]{0:T(1024)S(1)} %bitcast.49, f32[2048]{0:T(1024)S(1)} %bitcast.47, f32[2048]{0:T(1024)S(1)} %bitcast.51, f32[2048]{0:T(1024)S(1)} %bitcast.46, f32[48,2048]{1,0:T(8,128)S(1)} %get-tuple-element.232, ...), kind=kOutput, calls=%fused_computation.5.clone.1 | convolution fusion | flops 474152960 | bytes 1032197 | tf_op jit(solution)/shard_map/while/body/eval_jaxpr/dot_general | solution.py:72
  399.4 1.0 constant_dynamic-slice_fusion.2
  400.4 14.2 %fusion.26 = f32[48,2048]{1,0:T(8,128)S(1)} fusion(f32[2048]{0:T(1024)S(1)} %bitcast.50, f32[2048]{0:T(1024)S(1)} %bitcast.48, f32[2048]{0:T(1024)S(1)} %bitcast.49, f32[2048]{0:T(1024)S(1)} %bitcast.47, f32[2048]{0:T(1024)S(1)} %bitcast.51, f32[2048]{0:T(1024)S(1)} %bitcast.46, f32[48,2048]{1,0:T(8,128)S(1)} %get-tuple-element.232, ...), kind=kOutput, calls=%fused_computation.5.clone.1 | convolution fusion | flops 474152960 | bytes 1032197 | tf_op jit(solution)/shard_map/while/body/eval_jaxpr/dot_general | solution.py:72
  414.6 0.0 copy-start.1
  414.6 0.7 copy-done.1
  (7 shorter events, 0.1 us)
Async XLA Ops:
  10.3 11.0 %all-to-all-start = ((s32[32,16,1]{1,2,0:T(1,128)}), s32[32,16,1]{1,2,0:T(1,128)S(1)}, u32[]{:S(2)}, u32[]{:S(2)}) async-start(s32[32,16,1]{1,2,0:T(1,128)} %bitcast.2), calls=%async_computation | async-start | bytes 32768 | tf_op jit(solution)/shard_map/all_to_all | solution.py:46
  21.3 10.7 %all-to-all-start.1 = ((f32[32,1,768]{2,1,0:T(1,128)}), f32[32,1,768]{2,1,0:T(1,128)S(1)}, u32[]{:S(2)}, u32[]{:S(2)}) async-start(f32[32,1,768]{2,1,0:T(1,128)} %reshape.94), calls=%async_computation.1 | async-start | bytes 196608 | tf_op jit(solution)/shard_map/all_to_all | solution.py:45
  26.2 145.7 %all-gather.2.cloned.1.call-start = ((), (), s32[]{:S(2)}) async-start(), calls=%async_computation.2 | async-start | bytes 3538944 | tf_op jit(solution)/shard_map/all_gather | solution.py:63
  58.9 113.0 %copy-start = (f32[3,2048]{1,0:T(4,128)S(1)}, f32[3,2048]{1,0:T(4,128)}, u32[]{:S(2)}) copy-start(f32[3,2048]{1,0:T(4,128)} %param.11) | copy-start | bytes 73732
  414.6 0.7 copy-start.1
Sparse Core Ops, SparseCore 0:
  110.7 61.1 all-gather.1
where the time goes:
time: 428 us; the launch traced here: 422 us
  matrix products  253 us (59%)
  waiting for transfers between devices  67.3 us (16%)
  blocking collectives  47.2 us (11%)
  local copies, waits for them, and re-layouts  23.2 us (5%)
  between operations  13.5 us (3%)
  starting transfers between devices  11.3 us (3%)
  other arithmetic  5.97 us (1%)
    dot_general x16, matrix products, one_block(): jnp.dot(coef_part, kernel_tile, preferred_element_type=jnp.float32)  226 us
    all_gather x1, waiting for transfers between devices, per_device(): shard_piece = lax.all_gather(coef_bf, 'row', axis=1, tiled=True)  61.3 us
    dot_general x1, matrix products, per_device(): lax.dot_general(lax.all_gather(disp_bf, 'row', axis=1, tiled=True), inver...  26.7 us
    psum x1, blocking collectives, per_device(): summed = lax.psum(partial_value, 'col')  25 us
    all_gather x1, blocking collectives, per_device(): lax.all_gather(disp_bf, 'row', axis=1, tiled=True)  22.3 us
    slice x16, local copies, waits for them, and re-layouts, wendland_tile(): centre_block[component][:, None] - node_block[component][None, :]  15.7 us
  transfers between devices with their start and end apart: 3, of which 3 were waited for; matrix products, arithmetic and copies ran while one was open for 1% of the time, Pallas kernels for 0%

commit v1 on v0

v1 whole, which is shorter than its diff:
```python
import functools
import math

import jax
import jax.numpy as jnp
from jax import lax
from jax.experimental import pallas as pl
from jax.experimental.pallas import tpu as pltpu
from jax.sharding import PartitionSpec as P

M = 32768
RADIUS = 2.0 / math.sqrt(M)
GROUP = 8
CHUNK = 128
BATCH = 32
CELL_BITS = 5


def split_three(values):
    first = lax.reduce_precision(values, 8, 7)
    rest = values - first
    second = lax.reduce_precision(rest, 8, 7)
    third = rest - second
    return jnp.concatenate([first, second, third], axis=0).astype(jnp.bfloat16)


def join_three(stacked):
    rows = stacked.shape[0] // 3
    return stacked[:rows] + stacked[rows : 2 * rows] + stacked[2 * rows :]


def place_key(points):
    centred = points - 0.5
    size = jnp.abs(centred)
    x, y, z = size[0], size[1], size[2]
    on_x = (x >= y) & (x >= z)
    on_y = jnp.logical_not(on_x) & (y >= z)
    axis = jnp.where(on_x, 0, jnp.where(on_y, 1, 2))
    normal = jnp.where(on_x, centred[0], jnp.where(on_y, centred[1], centred[2]))
    u = jnp.where(on_x, points[1], points[0])
    v = jnp.where(on_x | on_y, points[2], points[1])
    cells = 1 << CELL_BITS
    iu = jnp.clip(jnp.floor((u - 0.3) * (cells / 0.4)), 0, cells - 1).astype(jnp.int32)
    iv = jnp.clip(jnp.floor((v - 0.3) * (cells / 0.4)), 0, cells - 1).astype(jnp.int32)
    code = axis * 2 + (normal > 0).astype(jnp.int32)
    for bit in reversed(range(CELL_BITS)):
        code = code * 4 + ((iu >> bit) & 1) * 2 + ((iv >> bit) & 1)
    return code


def ranks(points):
    count = points.shape[1]
    key = place_key(points) * count + jnp.arange(count, dtype=jnp.int32)
    return jnp.sum((key[:, None] < key[None, :]).astype(jnp.int32), axis=0)


def one_hot(ids, first, count):
    wanted = first + jnp.arange(count, dtype=jnp.int32)
    return (wanted[:, None] == ids[None, :]).astype(jnp.bfloat16)


def times_rows(left, right):
    return lax.dot_general(
        left, right, (((1,), (1,)), ((), ())), preferred_element_type=jnp.float32
    )


def volume_kernel(chunks, groups, counts, lists, centres, nodes, coefs, out, spread):
    total = groups + 1

    def spread_one(g, carry):
        rows = pl.ds(pl.multiple_of(g * GROUP, GROUP), GROUP)
        block = nodes[rows, :]
        for d in range(3):
            spread[d, rows, :] = jnp.broadcast_to(block[:, d : d + 1], (GROUP, 128))
        return carry

    lax.fori_loop(0, total, spread_one, 0)
    out[...] = jnp.zeros_like(out)

    def one_chunk(c, carry):
        columns = pl.ds(pl.multiple_of(c * CHUNK, CHUNK), CHUNK)
        here = [centres[d : d + 1, columns] for d in range(3)]
        coef = coefs[:, columns]

        def one_batch(b, inner):
            tiles = []
            starts = []
            for g in range(BATCH):
                start = pl.multiple_of(lists[c, b * BATCH + g] * GROUP, GROUP)
                starts.append(start)
                squared = None
                for d in range(3):
                    difference = spread[d, pl.ds(start, GROUP), :] - here[d]
                    term = difference * difference
                    squared = term if squared is None else squared + term
                scaled = jnp.sqrt(squared)
                remain = jnp.maximum(1.0 - scaled, 0.0)
                remain = remain * remain
                remain = remain * remain
                tiles.append(remain * (4.0 * scaled + 1.0))
            phi = jnp.concatenate(tiles, axis=0).astype(jnp.bfloat16)
            product = times_rows(phi, coef)
            for g in range(BATCH):
                rows = pl.ds(starts[g], GROUP)
                out[rows, :] += product[g * GROUP : (g + 1) * GROUP]
            return inner

        batches = (counts[c] + (BATCH - 1)) // BATCH
        return lax.fori_loop(0, batches, one_batch, carry)

    lax.fori_loop(0, chunks, one_chunk, 0)


def volume(coefs, centres, nodes):
    centre_count = centres.shape[1]
    node_count = nodes.shape[1]
    chunks = centre_count // CHUNK
    groups = node_count // GROUP
    centre_boxes = centres.reshape(3, chunks, CHUNK)
    node_boxes = nodes.reshape(3, groups, GROUP)
    gap = jnp.maximum(
        jnp.min(centre_boxes, axis=2)[:, :, None] - jnp.max(node_boxes, axis=2)[:, None, :],
        jnp.min(node_boxes, axis=2)[:, None, :] - jnp.max(centre_boxes, axis=2)[:, :, None],
    )
    gap = jnp.maximum(gap, 0.0)
    near = jnp.sum(gap * gap, axis=0) <= RADIUS * RADIUS * 1.001
    near_f = near.astype(jnp.bfloat16)
    earlier = (jnp.arange(groups)[:, None] < jnp.arange(groups)[None, :]).astype(jnp.bfloat16)
    place = lax.dot_general(
        near_f, earlier, (((1,), (0,)), ((), ())), preferred_element_type=jnp.float32
    ).astype(jnp.int32)
    place = jnp.where(near, place, -1)
    counts = jnp.sum(near.astype(jnp.int32), axis=1)
    slots = -(-groups // BATCH) * BATCH
    hit = place[:, None, :] == jnp.arange(slots, dtype=jnp.int32)[None, :, None]
    lists = groups + jnp.sum(
        jnp.where(hit, jnp.arange(groups, dtype=jnp.int32)[None, None, :] - groups, 0), axis=2
    )
    scale = 1.0 / RADIUS
    far = jnp.full((GROUP, 3), 1e4, jnp.float32)
    node_rows = jnp.concatenate([nodes.T * scale, far], axis=0)
    smem = pl.BlockSpec(memory_space=pltpu.SMEM)
    vmem = pl.BlockSpec(memory_space=pltpu.VMEM)
    result = pl.pallas_call(
        functools.partial(volume_kernel, chunks, groups),
        out_shape=jax.ShapeDtypeStruct((node_count + GROUP, coefs.shape[0]), jnp.float32),
        in_specs=[smem, smem, vmem, vmem, vmem],
        out_specs=vmem,
        scratch_shapes=[pltpu.VMEM((3, node_count + GROUP, 128), jnp.float32)],
        compiler_params=pltpu.CompilerParams(vmem_limit_bytes=40 * 1024 * 1024),
        name="volume",
    )(counts, lists, centres * scale, node_rows, coefs)
    return result[:node_count]


def per_device(struct_disp, target, inverse, centre_xyz, node_xyz):
    row_count = lax.axis_size("row")
    col_count = lax.axis_size("col")
    owner_count = row_count * col_count
    row_at = lax.axis_index("row")
    col_at = lax.axis_index("col")
    row_block, col_block = inverse.shape
    owner_block = row_block // col_count
    own_piece = row_block // col_count
    disp_rows, entries = struct_disp.shape

    slot_cap = max(2, 2 * entries // owner_count)
    owner_ids = target % col_block // owner_block * col_count + target // col_block
    offsets = target % owner_block
    at = jnp.arange(entries, dtype=jnp.int32)
    same = (owner_ids[:, None] == owner_ids[None, :]) & (at[:, None] < at[None, :])
    ranking = jnp.sum(same.astype(jnp.int32), axis=0)
    slot_ids = owner_ids * slot_cap + ranking
    pick = one_hot(slot_ids, 0, owner_count * slot_cap)
    outgoing = jnp.concatenate([struct_disp, offsets.astype(jnp.float32)[None, :] + 1.0], axis=0)
    sent = times_rows(pick, split_three(outgoing))
    width = disp_rows + 1
    sent = sent[:, :width] + sent[:, width : 2 * width] + sent[:, 2 * width :]
    received = lax.all_to_all(sent, ("row", "col"), split_axis=0, concat_axis=0, tiled=True)
    recv_offsets = received[:, disp_rows].astype(jnp.int32) - 1
    spots = one_hot(recv_offsets, 0, owner_block)
    centre_disp = join_three(times_rows(split_three(received[:, :disp_rows].T), spots))
    disp_bf = centre_disp.astype(jnp.bfloat16)
    disp_block = lax.all_gather(disp_bf, "row", axis=1, tiled=True)

    mine = lax.dynamic_slice_in_dim(centre_xyz, row_at * row_block, row_block, 1)
    order = one_hot(ranks(mine), col_at * own_piece, own_piece)
    placed_xyz = join_three(times_rows(split_three(mine), order))
    centres = lax.all_gather(placed_xyz, ("row", "col"), axis=1, tiled=True)
    node_order = one_hot(ranks(node_xyz), 0, node_xyz.shape[1])
    nodes = join_three(times_rows(split_three(node_xyz), node_order))

    partial_value = times_rows(disp_block, inverse)
    coef_bf = lax.psum(partial_value, "col").astype(jnp.bfloat16)
    placed_coefs = times_rows(coef_bf, order).astype(jnp.bfloat16)
    coefs = lax.all_gather(placed_coefs, ("row", "col"), axis=1, tiled=True)
    result = volume(coefs, centres, nodes)
    back = lax.dot_general(
        split_three(result.T), node_order, (((1,), (0,)), ((), ())), preferred_element_type=jnp.float32
    )
    return join_three(back)


def solution(mesh):
    placed = (
        P(None, ("row", "col")),
        P(("row", "col")),
        P("row", "col"),
        P(),
        P(None, ("row", "col")),
    )
    return jax.shard_map(
        per_device, mesh=mesh, in_specs=placed, out_specs=P(None, ("row", "col")), check_vma=False
    )
```

time: 428 us -> 471 us (1.10)
  matrix products: 253 us -> 41.4 us
  Pallas kernels: 0 us -> 208 us
  blocking collectives: 47.2 us -> 87.6 us
  other arithmetic: 5.97 us -> 40.6 us
  local copies, waits for them, and re-layouts: 23.2 us -> 4.95 us
  waiting for transfers between devices: 67.3 us -> 62 us
  starting transfers between devices: 11.3 us -> 6.34 us
    dot_general x17 -> x8, matrix products: 253 us -> 41.4 us  [the longest x6 36.9 us: times_rows(): lax.dot_general(left, right, (((1,), (1,)), ((), ())), preferred_element_...]
    pallas_call x0 -> x1, Pallas kernels: none -> 208 us  [volume(): pl.pallas_call(functools.partial(volume_kernel, chunks, groups), out_shap...]
    all_gather x1 -> x2, blocking collectives: 22.3 us -> 63.7 us  [the longest x1 33.4 us: per_device(): centres = lax.all_gather(placed_xyz, ('row', 'col'), axis=1, tiled=True)]
    reduce_sum x1 -> x6, other arithmetic: 0.1 us -> 29.3 us  [the longest x1 18.7 us: volume(): jnp.sum(jnp.where(hit, jnp.arange(groups, dtype=jnp.int32)[None, None, :]...]
    slice x16 -> x3, local copies, waits for them, and re-layouts: 15.7 us -> 0.95 us  [the longest x1 0.9 us: place_key(): u = jnp.where(on_x, points[1], points[0])]
    all_to_all x2 -> x1, waiting for transfers between devices: 5.98 us -> 0.01 us  [per_device(): lax.all_to_all(sent, ('row', 'col'), split_axis=0, concat_axis=0, tiled=T...]
    add x0 -> x12, other arithmetic: none -> 5.44 us  [the longest x4 2.48 us: ranks(): key = place_key(points) * count + jnp.arange(count, dtype=jnp.int32)]
    all_to_all x2 -> x1, starting transfers between devices: 11.3 us -> 6.3 us  [per_device(): lax.all_to_all(sent, ('row', 'col'), split_axis=0, concat_axis=0, tiled=T...]
  transfers between devices with their start and end apart: 3 -> 2, of which waited for: 3 -> 1; matrix products, arithmetic and copies ran while one was open for 1% -> 9% of each run, Pallas kernels for 0% -> 0%
where the time goes in v1:
time: 471 us; the launch traced here: 465 us
  Pallas kernels  208 us (44%)
  blocking collectives  87.6 us (19%)
  waiting for transfers between devices  62 us (13%)
  matrix products  41.4 us (9%)
  other arithmetic  40.6 us (9%)
  between operations  13.7 us (3%)
  starting transfers between devices  6.34 us (1%)
  local copies, waits for them, and re-layouts  4.95 us (1%)
    pallas_call x1, Pallas kernels, volume(): pl.pallas_call(functools.partial(volume_kernel, chunks, groups), out_shap...  208 us
    all_gather x1, waiting for transfers between devices, per_device(): coefs = lax.all_gather(placed_coefs, ('row', 'col'), axis=1, tiled=True)  62 us
    dot_general x6, matrix products, times_rows(): lax.dot_general(left, right, (((1,), (1,)), ((), ())), preferred_element_...  36.9 us
    all_gather x1, blocking collectives, per_device(): centres = lax.all_gather(placed_xyz, ('row', 'col'), axis=1, tiled=True)  33.4 us
    all_gather x1, blocking collectives, per_device(): disp_block = lax.all_gather(disp_bf, 'row', axis=1, tiled=True)  30.3 us
    psum x1, blocking collectives, per_device(): coef_bf = lax.psum(partial_value, 'col').astype(jnp.bfloat16)  23.9 us
    reduce_sum x1, other arithmetic, volume(): jnp.sum(jnp.where(hit, jnp.arange(groups, dtype=jnp.int32)[None, None, :]...  18.7 us
    reduce_sum x2, other arithmetic, ranks(): return jnp.sum((key[:, None] < key[None, :]).astype(jnp.int32), axis=0)  10 us
  transfers between devices with their start and end apart: 2, of which 1 were waited for; matrix products, arithmetic and copies ran while one was open for 9% of the time, Pallas kernels for 0%

profile of v1, /device:TPU:13, one launch (start us, length us, event | category | flops | bytes accessed | tf_op | source)
XLA Modules:
  0.0 464.6 jit_solution(6281990232725380438)
XLA Ops:
  6.5 0.7 fusion.63
  7.2 0.7 convert_add_fusion
  7.9 0.1 convert_reduce_fusion.2
  8.0 0.7 multiply_add_fusion
  8.7 0.8 reduce-precision_convert_fusion.7
  9.6 0.3 fusion.24
  9.9 0.1 copy.34
  10.0 0.9 reshape.294
  10.9 6.3 %all-to-all-start = ((f32[32,1,784]{2,1,0:T(1,128)}), f32[32,1,784]{2,1,0:T(1,128)S(1)}, u32[]{:S(2)}, u32[]{:S(2)}) async-start(f32[32,1,784]{2,1,0:T(1,128)} %reshape.294), calls=%async_computation | async-start | bytes 229376 | tf_op jit(solution)/shard_map/all_to_all | solution.py:180
  17.3 0.0 all-gather.2.cloned.1.call-start
  17.3 0.8 reduce-precision_convert_fusion.9
  18.1 0.9 fusion.77
  19.0 0.1 fusion.73
  19.1 0.9 reduce-precision_convert_fusion.5
  20.0 0.1 fusion.70
  20.2 1.3 iota_add_fusion
  21.5 0.1 iota_add_fusion.1
  21.6 8.3 %convert_reduce_fusion = s32[4096]{0:T(1024)S(1)} fusion(s32[4096]{0:T(1024)S(1)} %bitcast.64, s32[4096]{0:T(1024)S(1)} %iota_add_fusion.1), kind=kLoop, calls=%fused_computation.2 | loop fusion | flops 50327552 | bytes 49152 | tf_op jit(solution)/shard_map/reduce_sum | solution.py:54
  30.0 2.7 fusion.2
  32.7 33.4 %all_gather.9 = f32[3,32768]{1,0:T(4,128)S(1)} all-gather(f32[3,1024]{1,0:T(4,128)S(1)} %slice_add_fusion.8), channel_id=1, replica_groups=mesh['row'=8,'col'=4] {'row','col'}, dimensions={1}, use_global_device_ids=true | all-gather | bytes 405504 | tf_op jit(solution)/shard_map/all_gather | solution.py:190
  66.1 0.3 bitcast_reduce_fusion.3
  66.3 1.1 iota_add_fusion.2
  67.4 1.7 convert_reduce_fusion.1
  69.1 3.0 fusion.5
  72.1 0.6 multiply_bitcast_fusion
  72.8 0.6 bitcast_reduce_fusion.1
  73.4 0.1 copy.33
  73.5 0.1 copy.32
  73.6 0.3 multiply_reduce_fusion
  73.8 0.1 convert_reduce_fusion.3
  74.0 0.2 fusion.13
  74.2 18.7 %select_reduce_fusion = s32[256,256]{1,0:T(8,128)S(1)} fusion(s32[256]{0:T(256)S(1)} %iota_add_fusion.5, s32[256,256]{1,0:T(8,128)S(1)} %fusion.13), kind=kLoop, calls=%fused_computation | loop fusion | flops 50266112 | bytes 525312 | tf_op jit(solution)/shard_map/reduce_sum | solution.py:137
  92.9 0.1 concatenate.28.nodes
  93.0 0.0 all-to-all-done
  93.0 0.5 broadcast.611
  93.5 0.9 reduce.10
  94.4 0.2 reshape.295
  94.6 0.2 fusion.27
  94.9 0.1 copy.37
  95.0 0.6 fusion.12
  95.6 30.3 %all_gather.10 = bf16[48,8192]{1,0:T(8,128)(2,1)S(1)} all-gather(bf16[48,1024]{1,0:T(8,128)(2,1)S(1)} %fusion.30), channel_id=1, replica_groups=mesh['row'=8,'col'=4] {'row'}, dimensions={1}, use_global_device_ids=true | all-gather | bytes 884736 | tf_op jit(solution)/shard_map/all_gather | solution.py:185
  125.9 26.8 %fusion.78 = f32[48,4096]{1,0:T(8,128)S(1)} fusion(bf16[48,8192]{1,0:T(8,128)(2,1)S(1)} %all_gather.10, bf16[4096,8192]{1,0:T(8,128)(2,1)} %param.7), kind=kOutput, calls=%fused_computation.163 | convolution fusion | flops 3221225472 | bytes 68681728 | tf_op jit(solution)/shard_map/dot_general | solution.py:63
  152.7 23.9 %all-reduce.2 = bf16[48,4096]{1,0:T(8,128)(2,1)S(1)} all-reduce(f32[48,4096]{1,0:T(8,128)S(1)} %fusion.78), channel_id=1, replica_groups=mesh['row'=8,'col'=4] {'col'}, use_global_device_ids=true, to_apply=%region_10.11 | all-reduce | flops 196608 | bytes 1179648 | tf_op jit(solution)/shard_map/psum | solution.py:195
  176.6 3.6 fusion.14
  180.2 0.0 all-gather.2.cloned.1.call-update
  180.3 0.1 broadcast_multiply_fusion.centres
  180.4 62.0 %all-gather.2.cloned.1.call-done.coefs = bf16[48,32768]{1,0:T(8,128)(2,1)} async-done(((bf16[48,1024]{1,0:T(8,128)(2,1)}), bf16[48,32768]{1,0:T(8,128)(2,1)}) %all-gather.2.cloned.1.call-update) | async-done | bytes 3145744 | tf_op jit(solution)/shard_map/all_gather | solution.py:197
  242.4 0.0 copy-start
  242.4 1.9 copy-done
  244.3 208.1 %volume.1 = f32[2056,48]{1,0:T(8,128)S(1)} custom-call(s32[256]{0:T(256)S(1)} %get-tuple-element.11.counts, s32[256,256]{1,0:T(8,128)S(1)} %broadcast_add_fusion.lists, f32[3,32768]{1,0:T(4,128)S(1)} %broadcast_multiply_fusion.centres, f32[2056,3]{1,0:T(8,128)S(1)} %concatenate.28.nodes, bf16[48,32768]{1,0:T(8,128)(2,1)S(1)} %copy-done), custom_call_target="tpu_custom_call" | custom-call | tf_op jit(solution)/shard_map/volume/pallas_call | solution.py:145
  452.3 0.3 reduce-precision_convert_fusion.1
  452.6 4.3 fusion.4
  456.9 0.8 slice_add_fusion.2
  (10 shorter events, 0.2 us)
Async XLA Ops:
  10.9 82.0 %all-to-all-start = ((f32[32,1,784]{2,1,0:T(1,128)}), f32[32,1,784]{2,1,0:T(1,128)S(1)}, u32[]{:S(2)}, u32[]{:S(2)}) async-start(f32[32,1,784]{2,1,0:T(1,128)} %reshape.294), calls=%async_computation | async-start | bytes 229376 | tf_op jit(solution)/shard_map/all_to_all | solution.py:180
  17.3 225.1 %all-gather.2.cloned.1.call-start = ((), (), s32[]{:S(2)}) async-start(), calls=%async_computation.1 | async-start | bytes 3244032 | tf_op jit(solution)/shard_map/all_gather | solution.py:197
  242.4 1.9 copy-start
Sparse Core Ops, SparseCore 0:
  180.4 61.9 all-gather.1

commit v2 on v1

--- a/solution.py
+++ b/solution.py
@@ -13,6 +13,7 @@
 GROUP = 8
 CHUNK = 128
 BATCH = 32
+SUB = 16
 CELL_BITS = 5
 
 
@@ -65,8 +66,144 @@
     )
 
 
-def volume_kernel(chunks, groups, counts, lists, centres, nodes, coefs, out, spread):
+def gather_kernel(sizes, plans, pair_up, block, out, send_sem, recv_sem):
+    z_size, y_size, x_size = sizes
+    row_at = lax.axis_index("row")
+    col_at = lax.axis_index("col")
+    at = {
+        "z": lax.div(row_at, y_size),
+        "y": lax.rem(row_at, y_size),
+        "x": lax.div(col_at, 2),
+        "k": lax.rem(col_at, 2),
+    }
+    lengths = {"z": z_size, "y": y_size, "x": x_size, "k": 2}
+    used = ["z", "y", "x"] if pair_up else ["z", "y"]
+
+    def moved(axis, step):
+        place = dict(at)
+        place[axis] = lax.rem(at[axis] + step, lengths[axis])
+        return place
+
+    def device(place):
+        return (place["z"] * y_size + place["y"], place["x"] * 2 + place["k"])
+
+    partners = [(axis, step) for axis in used for step in range(1, lengths[axis])]
+    if pair_up:
+        partners.append(("k", 1))
+    barrier = pltpu.get_barrier_semaphore()
+    for axis, step in partners:
+        pl.semaphore_signal(
+            barrier, inc=1, device_id=device(moved(axis, step)), device_id_type=pl.DeviceIdType.MESH
+        )
+    pl.semaphore_wait(barrier, len(partners))
+
+    def slab(place, columns):
+        index = tuple(slice(None) if place[axis] is None else place[axis] for axis in used)
+        if pair_up:
+            index = index + (at["k"],)
+        return out.at[index + (slice(None), columns)]
+
+    out[tuple(at[axis] for axis in used) + ((at["k"],) if pair_up else ())] = block[...]
+    unsent = []
+    unmet = []
+    count = 0
+
+    def push(place, columns, axis, step):
+        nonlocal count
+        region = slab(place, columns)
+        copy = pltpu.make_async_remote_copy(
+            src_ref=region,
+            dst_ref=region,
+            send_sem=send_sem.at[count],
+            recv_sem=recv_sem.at[count],
+            device_id=device(moved(axis, step)),
+            device_id_type=pl.DeviceIdType.MESH,
+        )
+        copy.start()
+        count += 1
+        unsent.append(copy)
+        return copy
+
+    width = out.shape[-1] // len(plans)
+    parts = [slice(i * width, (i + 1) * width) for i in range(len(plans))]
+    held = [dict(at) for _ in plans]
+    for stage in range(len(used)):
+        copies = []
+        for part, plan in enumerate(plans):
+            axis = plan[stage]
+            for step in range(1, lengths[axis]):
+                copies.append((part, axis, step, push(held[part], parts[part], axis, step)))
+        if stage == 0 and pair_up:
+            for part in range(len(plans)):
+                unmet.append(push(held[part], parts[part], "k", 1))
+        for part, axis, step, copy in copies:
+            copy.wait_recv()
+            if pair_up:
+                place = dict(held[part])
+                place[axis] = lax.rem(at[axis] - step + lengths[axis], lengths[axis])
+                unmet.append(push(place, parts[part], "k", 1))
+        for part, plan in enumerate(plans):
+            held[part][plan[stage]] = None
+    for copy in unmet:
+        copy.wait_recv()
+    for copy in unsent:
+        copy.wait_send()
+
+
+def gather(block, row_count, col_count, plans, pair_up, collective_id):
+    y_size = 2 if row_count % 2 == 0 else 1
+    sizes = (row_count // y_size, y_size, col_count // 2)
+    leading = (*sizes, 2) if pair_up else sizes[:2]
+    stages = 3 if pair_up else 2
+    hops = sum(sizes[:stages]) - stages
+    copies = len(plans) * (2 * hops + 1)
+    vmem = pl.BlockSpec(memory_space=pltpu.VMEM)
+    out = pl.pallas_call(
+        functools.partial(gather_kernel, sizes, plans, pair_up),
+        out_shape=jax.ShapeDtypeStruct((*leading, *block.shape), block.dtype),
+        in_specs=[vmem],
+        out_specs=vmem,
+        scratch_shapes=[pltpu.SemaphoreType.DMA((copies,)), pltpu.SemaphoreType.DMA((copies,))],
+        compiler_params=pltpu.CompilerParams(
+            collective_id=collective_id,
+            has_side_effects=True,
+            vmem_limit_bytes=24 * 1024 * 1024,
+        ),
+        name="gather",
+    )(block)
+    return out.reshape(math.prod(leading), *block.shape)
+
+
+def compact_kernel(place_ref, lists):
+    place = place_ref[...]
+    width = place.shape[1]
+    group = lax.broadcasted_iota(jnp.int32, place.shape, 1)
+    value = jnp.where(place >= 0, (group - place) * 2 * width + group, -1)
+    step = 1
+    while step < width:
+        shifted = pltpu.roll(value, width - step, 1)
+        bit = step * 2 * width
+        arrives = (shifted >= 0) & ((shifted & bit) != 0)
+        stays = (value >= 0) & ((value & bit) == 0)
+        value = jnp.where(arrives, shifted, jnp.where(stays, value, -1))
+        step *= 2
+    lists[...] = jnp.where(value >= 0, value & (2 * width - 1), width)
+
+
+def volume_kernel(groups, counts, lists, centres, nodes, coefs, out, spread, items):
     total = groups + 1
+    chunks = counts.shape[0]
+    per_block = coefs.shape[2] // CHUNK
+    batches = groups // BATCH
+
+    def list_chunk(c, count):
+        def list_one(b, n):
+            items[n] = c * batches + b
+            return n + 1
+
+        return lax.fori_loop(0, (counts[c] + (BATCH - 1)) // BATCH, list_one, count)
+
+    item_count = lax.fori_loop(0, chunks, list_chunk, 0)
 
     def spread_one(g, carry):
         rows = pl.ds(pl.multiple_of(g * GROUP, GROUP), GROUP)
@@ -78,76 +215,96 @@
     lax.fori_loop(0, total, spread_one, 0)
     out[...] = jnp.zeros_like(out)
 
-    def one_chunk(c, carry):
+    def evaluate(item, live):
+        c = lax.div(item, batches)
+        b = lax.rem(item, batches)
         columns = pl.ds(pl.multiple_of(c * CHUNK, CHUNK), CHUNK)
-        here = [centres[d : d + 1, columns] for d in range(3)]
-        coef = coefs[:, columns]
-
-        def one_batch(b, inner):
-            tiles = []
-            starts = []
-            for g in range(BATCH):
-                start = pl.multiple_of(lists[c, b * BATCH + g] * GROUP, GROUP)
-                starts.append(start)
-                squared = None
-                for d in range(3):
-                    difference = spread[d, pl.ds(start, GROUP), :] - here[d]
-                    term = difference * difference
-                    squared = term if squared is None else squared + term
-                scaled = jnp.sqrt(squared)
-                remain = jnp.maximum(1.0 - scaled, 0.0)
-                remain = remain * remain
-                remain = remain * remain
-                tiles.append(remain * (4.0 * scaled + 1.0))
-            phi = jnp.concatenate(tiles, axis=0).astype(jnp.bfloat16)
-            product = times_rows(phi, coef)
-            for g in range(BATCH):
-                rows = pl.ds(starts[g], GROUP)
-                out[rows, :] += product[g * GROUP : (g + 1) * GROUP]
-            return inner
-
-        batches = (counts[c] + (BATCH - 1)) // BATCH
-        return lax.fori_loop(0, batches, one_batch, carry)
-
-    lax.fori_loop(0, chunks, one_chunk, 0)
-
-
-def volume(coefs, centres, nodes):
+        here = [jnp.broadcast_to(centres[d : d + 1, columns], (GROUP, CHUNK)) for d in range(3)]
+        within = pl.ds(pl.multiple_of(lax.rem(c, per_block) * CHUNK, CHUNK), CHUNK)
+        coef = coefs[lax.div(c, per_block), :, within]
+        tiles = []
+        starts = []
+        for g in range(BATCH):
+            group = lists[c, b * BATCH + g]
+            if live is not None:
+                group = jnp.where(live, group, groups)
+            start = pl.multiple_of(group * GROUP, GROUP)
+            starts.append(start)
+            squared = None
+            for d in range(3):
+                difference = spread[d, pl.ds(start, GROUP), :] - here[d]
+                term = difference * difference
+                squared = term if squared is None else squared + term
+            squared = jnp.maximum(squared, 1e-30)
+            scaled = squared * lax.rsqrt(squared)
+            remain = jnp.maximum(1.0 - scaled, 0.0)
+            remain = remain * remain
+            remain = remain * remain
+            tiles.append(remain * (4.0 * scaled + 1.0))
+        phi = jnp.concatenate(tiles, axis=0).astype(jnp.bfloat16)
+        return starts, times_rows(phi, coef)
+
+    def add_up(starts, product):
+        for g in range(BATCH):
+            rows = pl.ds(starts[g], GROUP)
+            out[rows, :] += product[g * GROUP : (g + 1) * GROUP]
+
+    def two_items(n, carry):
+        second = 2 * n + 1
+        live = second < item_count
+        first_starts, first_product = evaluate(items[2 * n], None)
+        second_starts, second_product = evaluate(items[jnp.minimum(second, item_count - 1)], live)
+        add_up(first_starts, first_product)
+        add_up(second_starts, second_product)
+        return carry
+
+    lax.fori_loop(0, (item_count + 1) // 2, two_items, 0)
+
+
+def volume_lists(centres, nodes):
     centre_count = centres.shape[1]
-    node_count = nodes.shape[1]
     chunks = centre_count // CHUNK
-    groups = node_count // GROUP
-    centre_boxes = centres.reshape(3, chunks, CHUNK)
+    groups = nodes.shape[1] // GROUP
+    centre_boxes = centres.reshape(3, centre_count // SUB, SUB)
     node_boxes = nodes.reshape(3, groups, GROUP)
     gap = jnp.maximum(
         jnp.min(centre_boxes, axis=2)[:, :, None] - jnp.max(node_boxes, axis=2)[:, None, :],
         jnp.min(node_boxes, axis=2)[:, None, :] - jnp.max(centre_boxes, axis=2)[:, :, None],
     )
     gap = jnp.maximum(gap, 0.0)
-    near = jnp.sum(gap * gap, axis=0) <= RADIUS * RADIUS * 1.001
-    near_f = near.astype(jnp.bfloat16)
+    least = jnp.min(jnp.sum(gap * gap, axis=0).reshape(chunks, CHUNK // SUB, groups), axis=1)
+    near = least <= RADIUS * RADIUS * 1.001
     earlier = (jnp.arange(groups)[:, None] < jnp.arange(groups)[None, :]).astype(jnp.bfloat16)
     place = lax.dot_general(
-        near_f, earlier, (((1,), (0,)), ((), ())), preferred_element_type=jnp.float32
+        near.astype(jnp.bfloat16), earlier, (((1,), (0,)), ((), ())), preferred_element_type=jnp.float32
     ).astype(jnp.int32)
-    place = jnp.where(near, place, -1)
     counts = jnp.sum(near.astype(jnp.int32), axis=1)
-    slots = -(-groups // BATCH) * BATCH
-    hit = place[:, None, :] == jnp.arange(slots, dtype=jnp.int32)[None, :, None]
-    lists = groups + jnp.sum(
-        jnp.where(hit, jnp.arange(groups, dtype=jnp.int32)[None, None, :] - groups, 0), axis=2
-    )
+    lists = pl.pallas_call(
+        compact_kernel,
+        out_shape=jax.ShapeDtypeStruct((chunks, groups), jnp.int32),
+        name="compact",
+    )(jnp.where(near, place, -1))
+    return counts, lists
+
+
+def volume(coefs, centres, nodes):
+    node_count = nodes.shape[1]
+    groups = node_count // GROUP
+    counts, lists = volume_lists(centres, nodes)
     scale = 1.0 / RADIUS
     far = jnp.full((GROUP, 3), 1e4, jnp.float32)
     node_rows = jnp.concatenate([nodes.T * scale, far], axis=0)
     smem = pl.BlockSpec(memory_space=pltpu.SMEM)
     vmem = pl.BlockSpec(memory_space=pltpu.VMEM)
     result = pl.pallas_call(
-        functools.partial(volume_kernel, chunks, groups),
-        out_shape=jax.ShapeDtypeStruct((node_count + GROUP, coefs.shape[0]), jnp.float32),
+        functools.partial(volume_kernel, groups),
+        out_shape=jax.ShapeDtypeStruct((node_count + GROUP, coefs.shape[1]), jnp.float32),
         in_specs=[smem, smem, vmem, vmem, vmem],
         out_specs=vmem,
-        scratch_shapes=[pltpu.VMEM((3, node_count + GROUP, 128), jnp.float32)],
+        scratch_shapes=[
+            pltpu.VMEM((3, node_count + GROUP, 128), jnp.float32),
+            pltpu.SMEM((counts.shape[0] * (groups // BATCH),), jnp.int32),
+        ],
         compiler_params=pltpu.CompilerParams(vmem_limit_bytes=40 * 1024 * 1024),
         name="volume",
     )(counts, lists, centres * scale, node_rows, coefs)
@@ -182,19 +339,24 @@
     spots = one_hot(recv_offsets, 0, owner_block)
     centre_disp = join_three(times_rows(split_three(received[:, :disp_rows].T), spots))
     disp_bf = centre_disp.astype(jnp.bfloat16)
-    disp_block = lax.all_gather(disp_bf, "row", axis=1, tiled=True)
+    halves = (("z", "y"), ("y", "z"))
+    disp_block = gather(disp_bf, row_count, col_count, halves, False, 1)
+    disp_block = disp_block.transpose(1, 0, 2).reshape(disp_rows, col_block)
 
     mine = lax.dynamic_slice_in_dim(centre_xyz, row_at * row_block, row_block, 1)
     order = one_hot(ranks(mine), col_at * own_piece, own_piece)
     placed_xyz = join_three(times_rows(split_three(mine), order))
-    centres = lax.all_gather(placed_xyz, ("row", "col"), axis=1, tiled=True)
+    placed_xyz = jnp.concatenate([placed_xyz, jnp.zeros((5, own_piece), jnp.float32)], axis=0)
+    centres = gather(placed_xyz, row_count, col_count, (("x", "y", "z"),), True, 2)
+    centres = centres[:, :3].transpose(1, 0, 2).reshape(3, centre_xyz.shape[1])
     node_order = one_hot(ranks(node_xyz), 0, node_xyz.shape[1])
     nodes = join_three(times_rows(split_three(node_xyz), node_order))
 
     partial_value = times_rows(disp_block, inverse)
     coef_bf = lax.psum(partial_value, "col").astype(jnp.bfloat16)
     placed_coefs = times_rows(coef_bf, order).astype(jnp.bfloat16)
-    coefs = lax.all_gather(placed_coefs, ("row", "col"), axis=1, tiled=True)
+    orders = (("x", "y", "z"), ("z", "x", "y"))
+    coefs = gather(placed_coefs, row_count, col_count, orders, True, 3)
     result = volume(coefs, centres, nodes)
     back = lax.dot_general(
         split_three(result.T), node_order, (((1,), (0,)), ((), ())), preferred_element_type=jnp.float32

time: 471 us -> 338 us (0.72)
  blocking collectives: 87.6 us -> 20.5 us
  waiting for transfers between devices: 62 us -> 0.01 us
  Pallas kernels: 208 us -> 226 us
  between operations: 13.7 us -> 0.36 us
  other arithmetic: 40.6 us -> 30.5 us
    all_gather x2 -> x0, blocking collectives: 63.7 us -> none  [the longest x1 33.4 us: per_device(): centres = lax.all_gather(placed_xyz, ('row', 'col'), axis=1, tiled=True)]
    all_gather x1 -> x0, waiting for transfers between devices: 62 us -> none  [per_device(): coefs = lax.all_gather(placed_coefs, ('row', 'col'), axis=1, tiled=True)]
    pallas_call x1 -> x5, Pallas kernels: 208 us -> 226 us  [the longest x1 155 us: volume(): pl.pallas_call(functools.partial(volume_kernel, groups), out_shape=jax.Sh...]
    reduce_sum x3 -> x2, other arithmetic: 19.1 us -> 2.21 us  [the longest x1 2.09 us: volume_lists(): jnp.sum(gap * gap, axis=0).reshape(chunks, CHUNK // SUB, groups)]
  transfers between devices with their start and end apart: 2 -> 1, of which waited for: 1 -> 0; matrix products, arithmetic and copies ran while one was open for 9% -> 11% of each run, Pallas kernels for 0% -> 7%
where the time goes in v2:
time: 338 us; the launch traced here: 334 us
  Pallas kernels  226 us (67%)
  matrix products  42.5 us (13%)
  other arithmetic  30.5 us (9%)
  blocking collectives  20.5 us (6%)
  local copies, waits for them, and re-layouts  6.95 us (2%)
  starting transfers between devices  6.35 us (2%)
    pallas_call x1, Pallas kernels, volume(): pl.pallas_call(functools.partial(volume_kernel, groups), out_shape=jax.Sh...  155 us
    pallas_call x3, Pallas kernels, gather(): pl.pallas_call(functools.partial(gather_kernel, sizes, plans, pair_up), o...  68.9 us
    dot_general x6, matrix products, times_rows(): lax.dot_general(left, right, (((1,), (1,)), ((), ())), preferred_element_...  37.3 us
    psum x1, blocking collectives, per_device(): coef_bf = lax.psum(partial_value, 'col').astype(jnp.bfloat16)  20.5 us
    reduce_sum x2, other arithmetic, ranks(): return jnp.sum((key[:, None] < key[None, :]).astype(jnp.int32), axis=0)  10 us
  transfers between devices with their start and end apart: 1, of which 0 were waited for; matrix products, arithmetic and copies ran while one was open for 11% of the time, Pallas kernels for 7%

profile of v2, /device:TPU:13, one launch (start us, length us, event | category | flops | bytes accessed | tf_op | source)
XLA Modules:
  0.0 333.6 jit_solution(991107486692118879)
XLA Ops:
  0.0 0.7 fusion.63
  0.7 0.7 convert_add_fusion
  1.4 0.1 convert_reduce_fusion.2
  1.5 0.7 multiply_add_fusion
  2.2 0.8 reduce-precision_convert_fusion.7
  3.0 0.3 fusion.24
  3.3 0.1 copy.44
  3.5 0.9 reshape.307
  4.4 6.4 %all-to-all-start = ((f32[32,1,784]{2,1,0:T(1,128)}), f32[32,1,784]{2,1,0:T(1,128)}, u32[]{:S(2)}, u32[]{:S(2)}) async-start(f32[32,1,784]{2,1,0:T(1,128)} %reshape.307), calls=%async_computation | async-start | bytes 229376 | tf_op jit(solution)/shard_map/all_to_all | solution.py:337
  10.8 1.4 reduce-precision_convert_fusion.9
  12.2 1.5 fusion.78
  13.6 1.2 fusion.74
  14.9 0.0 copy-done.1
  14.9 0.6 fusion.77
  15.5 0.9 reduce-precision_convert_fusion.5
  16.4 0.1 fusion.71
  16.6 0.0 copy-start.4
  16.6 1.3 iota_add_fusion
  17.9 0.1 iota_add_fusion.1
  18.0 8.3 %convert_reduce_fusion = s32[4096]{0:T(1024)S(1)} fusion(s32[4096]{0:T(1024)S(1)} %bitcast.80, s32[4096]{0:T(1024)S(1)} %iota_add_fusion.1), kind=kLoop, calls=%fused_computation | loop fusion | flops 50327552 | bytes 49152 | tf_op jit(solution)/shard_map/reduce_sum | solution.py:55
  26.3 0.0 copy-start.6
  26.4 2.7 fusion.2
  29.1 20.9 %gather.3 = f32[4,2,2,2,8,1024]{5,4,3,2,1,0:T(8,128)S(1)} custom-call(f32[8,1024]{1,0:T(8,128)S(1)} %concatenate.30.block), custom_call_target="tpu_custom_call" | custom-call | tf_op jit(solution)/shard_map/gather/pallas_call | solution.py:161
  50.0 0.0 copy-done.4
  50.0 0.1 slice.159
  50.1 1.0 multiply_bitcast_fusion.1
  51.1 2.2 reshape_reshape.3
  53.3 2.3 fusion.70
  55.7 1.1 iota_add_fusion.2
  56.8 0.8 iota_add_fusion.3
  57.6 1.7 convert_reduce_fusion.1
  59.3 0.0 copy-start.2
  59.3 3.8 %fusion.5 = f32[9,2048]{0,1:T(8,128)S(1)} fusion(s32[2048]{0:T(1024)S(1)} %convert_reduce_fusion.1, bf16[3,2048]{1,0:T(4,128)(2,1)} %get-tuple-element.50, bf16[3,2048]{1,0:T(4,128)(2,1)} %get-tuple-element.52, bf16[3,2048]{1,0:T(4,128)(2,1)} %get-tuple-element.48), kind=kOutput, calls=%fused_computation.8 | convolution fusion | flops 79802368 | bytes 118784 | tf_op jit(solution)/shard_map/dot_general | solution.py:64
  63.1 0.6 multiply_bitcast_fusion
  63.7 0.6 bitcast_reduce_fusion.2
  64.3 0.1 copy.43
  64.4 0.1 copy.42
  64.5 0.0 copy-done.2
  64.5 2.1 multiply_reduce_fusion
  66.6 0.5 bitcast_reduce_fusion
  67.1 0.1 convert_reduce_fusion.3
  67.2 0.9 fusion.13.place_ref
  68.1 2.6 compact.1.lists
  70.8 0.3 copy.50
  71.0 0.1 concatenate.32.nodes
  71.1 0.0 all-to-all-done
  71.1 0.5 broadcast.604
  71.6 1.8 reduce.10
  73.5 0.2 reshape.308
  73.7 0.2 fusion.27
  73.9 0.1 copy.49
  74.0 0.6 fusion.12
  74.6 15.9 %gather.4 = bf16[4,2,48,1024]{3,2,1,0:T(8,128)(2,1)S(1)} custom-call(bf16[48,1024]{1,0:T(8,128)(2,1)S(1)} %fusion.30.block), custom_call_target="tpu_custom_call" | custom-call | tf_op jit(solution)/shard_map/gather/pallas_call | solution.py:161
  90.6 0.1 copy.51
  90.6 0.0 copy-start.5
  90.6 0.0 copy-start.7
  90.6 27.0 %fusion.79 = f32[48,4096]{1,0:T(8,128)S(1)} fusion(bf16[48,8192]{1,0:T(8,128)(2,1)S(1)} %bitcast.64, bf16[4096,8192]{1,0:T(8,128)(2,1)} %param.7), kind=kOutput, calls=%fused_computation.160 | convolution fusion | flops 3221225472 | bytes 68681728 | tf_op jit(solution)/shard_map/dot_general | solution.py:64
  117.7 20.5 %all-reduce.3 = bf16[48,4096]{1,0:T(8,128)(2,1)S(1)} all-reduce(f32[48,4096]{1,0:T(8,128)S(1)} %fusion.79), channel_id=1, replica_groups=mesh['row'=8,'col'=4] {'col'}, use_global_device_ids=true, to_apply=%region_10.11 | all-reduce | flops 196608 | bytes 1179648 | tf_op jit(solution)/shard_map/psum | solution.py:356
  138.3 3.0 fusion.14.block
  141.2 32.1 %gather.5 = bf16[4,2,2,2,48,1024]{5,4,3,2,1,0:T(8,128)(2,1)S(1)} custom-call(bf16[48,1024]{1,0:T(8,128)(2,1)S(1)} %fusion.14.block), custom_call_target="tpu_custom_call" | custom-call | tf_op jit(solution)/shard_map/gather/pallas_call | solution.py:161
  173.3 154.9 %volume.1 = f32[2056,48]{1,0:T(8,128)S(1)} custom-call(s32[256]{0:T(256)S(1)} %get-tuple-element.13.counts, s32[256,256]{1,0:T(8,128)S(1)} %copy-done, f32[3,32768]{1,0:T(4,128)S(1)} %bitcast.63, f32[2056,3]{1,0:T(8,128)S(1)} %concatenate.32.nodes, bf16[32,48,1024]{2,1,0:T(8,128)(2,1)S(1)} %bitcast.60), custom_call_target="tpu_custom_call" | custom-call | tf_op jit(solution)/shard_map/volume/pallas_call | solution.py:299
  328.2 0.3 reduce-precision_convert_fusion.1
  328.5 4.3 %fusion.4 = f32[144,2048]{1,0:T(8,128)S(1)} fusion(s32[2048]{0:T(1024)S(1)} %convert_reduce_fusion.1, bf16[48,2048]{0,1:T(8,128)(2,1)S(1)} %get-tuple-element.30, bf16[48,2048]{0,1:T(8,128)(2,1)S(1)} %get-tuple-element.31, bf16[48,2048]{0,1:T(8,128)(2,1)S(1)} %get-tuple-element.29), kind=kOutput, calls=%fused_computation.7 | convolution fusion | flops 1213923328 | bytes 1777664 | tf_op jit(solution)/shard_map/dot_general | solution.py:361
  332.8 0.8 slice_add_fusion.2
  (15 shorter events, 0.2 us)
Async XLA Ops:
  4.4 66.7 %all-to-all-start = ((f32[32,1,784]{2,1,0:T(1,128)}), f32[32,1,784]{2,1,0:T(1,128)}, u32[]{:S(2)}, u32[]{:S(2)}) async-start(f32[32,1,784]{2,1,0:T(1,128)} %reshape.307), calls=%async_computation | async-start | bytes 229376 | tf_op jit(solution)/shard_map/all_to_all | solution.py:337
  12.2 2.7 copy-start.1
  16.6 33.4 %copy-start.4 = (s32[1024]{0:T(1024)}, s32[1024]{0:T(1024)S(1)}, u32[]{:S(2)}) copy-start(s32[1024]{0:T(1024)S(1)} %iota_add_fusion.4) | copy-start | bytes 12292
  26.3 23.7 %copy-start.6 = (s32[4096]{0:T(1024)}, s32[4096]{0:T(1024)S(1)}, u32[]{:S(2)}) copy-start(s32[4096]{0:T(1024)S(1)} %convert_reduce_fusion) | copy-start | bytes 49156
  59.3 5.2 %copy-start.2 = (f32[3,2048]{1,0:T(4,128)S(1)}, f32[3,2048]{1,0:T(4,128)}, u32[]{:S(2)}) copy-start(f32[3,2048]{1,0:T(4,128)} %get-tuple-element.5) | copy-start | bytes 73732
  59.3 5.2 %copy-start.3 = (f32[3,2048]{1,0:T(4,128)S(1)}, f32[3,2048]{1,0:T(4,128)}, u32[]{:S(2)}) copy-start(f32[3,2048]{1,0:T(4,128)} %get-tuple-element.6) | copy-start | bytes 73732
  90.6 47.6 %copy-start.5 = (s32[1024]{0:T(1024)S(1)}, s32[1024]{0:T(1024)}, u32[]{:S(2)}) copy-start(s32[1024]{0:T(1024)} %copy-done.4) | copy-start | bytes 12292
  90.6 47.6 %copy-start.7 = (s32[4096]{0:T(1024)S(1)}, s32[4096]{0:T(1024)}, u32[]{:S(2)}) copy-start(s32[4096]{0:T(1024)} %copy-done.6) | copy-start | bytes 49156
  117.7 55.6 %copy-start = (s32[256,256]{1,0:T(8,128)S(1)}, s32[256,256]{1,0:T(8,128)}, u32[]{:S(2)}) copy-start(s32[256,256]{1,0:T(8,128)} %compact.1.lists) | copy-start | bytes 786436

commit v3 on v2

--- a/solution.py
+++ b/solution.py
@@ -12,9 +12,10 @@
 RADIUS = 2.0 / math.sqrt(M)
 GROUP = 8
 CHUNK = 128
-BATCH = 32
+BATCH = 24
+TOGETHER = 4
 SUB = 16
-CELL_BITS = 5
+LEVELS = 1024
 
 
 def split_three(values):
@@ -30,7 +31,7 @@
     return stacked[:rows] + stacked[rows : 2 * rows] + stacked[2 * rows :]
 
 
-def place_key(points):
+def place_key(points, strips):
     centred = points - 0.5
     size = jnp.abs(centred)
     x, y, z = size[0], size[1], size[2]
@@ -40,18 +41,20 @@
     normal = jnp.where(on_x, centred[0], jnp.where(on_y, centred[1], centred[2]))
     u = jnp.where(on_x, points[1], points[0])
     v = jnp.where(on_x | on_y, points[2], points[1])
-    cells = 1 << CELL_BITS
-    iu = jnp.clip(jnp.floor((u - 0.3) * (cells / 0.4)), 0, cells - 1).astype(jnp.int32)
-    iv = jnp.clip(jnp.floor((v - 0.3) * (cells / 0.4)), 0, cells - 1).astype(jnp.int32)
-    code = axis * 2 + (normal > 0).astype(jnp.int32)
-    for bit in reversed(range(CELL_BITS)):
-        code = code * 4 + ((iu >> bit) & 1) * 2 + ((iv >> bit) & 1)
-    return code
-
-
-def ranks(points):
+    strip = jnp.clip(jnp.floor((u - 0.3) * (strips / 0.4)), 0, strips - 1).astype(jnp.int32)
+    along = jnp.clip(jnp.floor((v - 0.3) * (LEVELS / 0.4)), 0, LEVELS - 1).astype(jnp.int32)
+    along = jnp.where(strip % 2 == 1, LEVELS - 1 - along, along)
+    face = axis * 2 + (normal > 0).astype(jnp.int32)
+    return (face * strips + strip) * LEVELS + along
+
+
+def even_strips(count, run):
+    return max(2, 2 * round(math.sqrt(count / 6 / run) / 2))
+
+
+def ranks(points, run):
     count = points.shape[1]
-    key = place_key(points) * count + jnp.arange(count, dtype=jnp.int32)
+    key = place_key(points, even_strips(count, run)) * count + jnp.arange(count, dtype=jnp.int32)
     return jnp.sum((key[:, None] < key[None, :]).astype(jnp.int32), axis=0)
 
 
@@ -124,8 +127,8 @@
         unsent.append(copy)
         return copy
 
-    width = out.shape[-1] // len(plans)
-    parts = [slice(i * width, (i + 1) * width) for i in range(len(plans))]
+    parts = [columns for _, columns in plans]
+    plans = [plan for plan, _ in plans]
     held = [dict(at) for _ in plans]
     for stage in range(len(used)):
         copies = []
@@ -150,7 +153,13 @@
         copy.wait_send()
 
 
-def gather(block, row_count, col_count, plans, pair_up, collective_id):
+def gather(block, row_count, col_count, orders, shares, pair_up, collective_id):
+    units = block.shape[1] // 128
+    if units % sum(shares) != 0:
+        orders, shares = (orders[-2:], (1, 1)) if units % 2 == 0 else (orders[-1:], (1,))
+    share = block.shape[1] // sum(shares)
+    edges = [sum(shares[:i]) * share for i in range(len(shares) + 1)]
+    plans = [(order, slice(edges[i], edges[i + 1])) for i, order in enumerate(orders)]
     y_size = 2 if row_count % 2 == 0 else 1
     sizes = (row_count // y_size, y_size, col_count // 2)
     leading = (*sizes, 2) if pair_up else sizes[:2]
@@ -194,7 +203,7 @@
     total = groups + 1
     chunks = counts.shape[0]
     per_block = coefs.shape[2] // CHUNK
-    batches = groups // BATCH
+    batches = lists.shape[1] // BATCH
 
     def list_chunk(c, count):
         def list_one(b, n):
@@ -204,6 +213,8 @@
         return lax.fori_loop(0, (counts[c] + (BATCH - 1)) // BATCH, list_one, count)
 
     item_count = lax.fori_loop(0, chunks, list_chunk, 0)
+    for n in range(TOGETHER - 1):
+        items[item_count + n] = chunks * batches
 
     def spread_one(g, carry):
         rows = pl.ds(pl.multiple_of(g * GROUP, GROUP), GROUP)
@@ -215,9 +226,10 @@
     lax.fori_loop(0, total, spread_one, 0)
     out[...] = jnp.zeros_like(out)
 
-    def evaluate(item, live):
-        c = lax.div(item, batches)
-        b = lax.rem(item, batches)
+    def evaluate(item):
+        row = lax.div(item, batches)
+        first = lax.rem(item, batches) * BATCH
+        c = jnp.minimum(row, chunks - 1)
         columns = pl.ds(pl.multiple_of(c * CHUNK, CHUNK), CHUNK)
         here = [jnp.broadcast_to(centres[d : d + 1, columns], (GROUP, CHUNK)) for d in range(3)]
         within = pl.ds(pl.multiple_of(lax.rem(c, per_block) * CHUNK, CHUNK), CHUNK)
@@ -225,10 +237,7 @@
         tiles = []
         starts = []
         for g in range(BATCH):
-            group = lists[c, b * BATCH + g]
-            if live is not None:
-                group = jnp.where(live, group, groups)
-            start = pl.multiple_of(group * GROUP, GROUP)
+            start = pl.multiple_of(lists[row, first + g] * GROUP, GROUP)
             starts.append(start)
             squared = None
             for d in range(3):
@@ -249,16 +258,13 @@
             rows = pl.ds(starts[g], GROUP)
             out[rows, :] += product[g * GROUP : (g + 1) * GROUP]
 
-    def two_items(n, carry):
-        second = 2 * n + 1
-        live = second < item_count
-        first_starts, first_product = evaluate(items[2 * n], None)
-        second_starts, second_product = evaluate(items[jnp.minimum(second, item_count - 1)], live)
-        add_up(first_starts, first_product)
-        add_up(second_starts, second_product)
+    def some_items(n, carry):
+        results = [evaluate(items[TOGETHER * n + i]) for i in range(TOGETHER)]
+        for starts, product in results:
+            add_up(starts, product)
         return carry
 
-    lax.fori_loop(0, (item_count + 1) // 2, two_items, 0)
+    lax.fori_loop(0, lax.div(item_count + (TOGETHER - 1), TOGETHER), some_items, 0)
 
 
 def volume_lists(centres, nodes):
@@ -284,7 +290,8 @@
         out_shape=jax.ShapeDtypeStruct((chunks, groups), jnp.int32),
         name="compact",
     )(jnp.where(near, place, -1))
-    return counts, lists
+    spare = -(-groups // BATCH) * BATCH - groups
+    return counts, jnp.pad(lists, ((0, 1), (0, spare)), constant_values=groups)
 
 
 def volume(coefs, centres, nodes):
@@ -303,7 +310,7 @@
         out_specs=vmem,
         scratch_shapes=[
             pltpu.VMEM((3, node_count + GROUP, 128), jnp.float32),
-            pltpu.SMEM((counts.shape[0] * (groups // BATCH),), jnp.int32),
+            pltpu.SMEM((counts.shape[0] * (lists.shape[1] // BATCH) + TOGETHER,), jnp.int32),
         ],
         compiler_params=pltpu.CompilerParams(vmem_limit_bytes=40 * 1024 * 1024),
         name="volume",
@@ -339,24 +346,25 @@
     spots = one_hot(recv_offsets, 0, owner_block)
     centre_disp = join_three(times_rows(split_three(received[:, :disp_rows].T), spots))
     disp_bf = centre_disp.astype(jnp.bfloat16)
-    halves = (("z", "y"), ("y", "z"))
-    disp_block = gather(disp_bf, row_count, col_count, halves, False, 1)
+    disp_orders = (("z", "y"), ("y", "z"))
+    disp_block = gather(disp_bf, row_count, col_count, disp_orders, (3, 1), False, 1)
     disp_block = disp_block.transpose(1, 0, 2).reshape(disp_rows, col_block)
 
     mine = lax.dynamic_slice_in_dim(centre_xyz, row_at * row_block, row_block, 1)
-    order = one_hot(ranks(mine), col_at * own_piece, own_piece)
+    order = one_hot(ranks(mine, CHUNK), col_at * own_piece, own_piece)
     placed_xyz = join_three(times_rows(split_three(mine), order))
-    placed_xyz = jnp.concatenate([placed_xyz, jnp.zeros((5, own_piece), jnp.float32)], axis=0)
-    centres = gather(placed_xyz, row_count, col_count, (("x", "y", "z"),), True, 2)
-    centres = centres[:, :3].transpose(1, 0, 2).reshape(3, centre_xyz.shape[1])
-    node_order = one_hot(ranks(node_xyz), 0, node_xyz.shape[1])
+    packed_xyz = placed_xyz.reshape(3 * own_piece // 128, 128)
+    centres = gather(packed_xyz, row_count, col_count, (("z", "x", "y"),), (1,), True, 2)
+    centres = centres.reshape(owner_count, 3, own_piece).transpose(1, 0, 2)
+    centres = centres.reshape(3, centre_xyz.shape[1])
+    node_order = one_hot(ranks(node_xyz, GROUP), 0, node_xyz.shape[1])
     nodes = join_three(times_rows(split_three(node_xyz), node_order))
 
     partial_value = times_rows(disp_block, inverse)
     coef_bf = lax.psum(partial_value, "col").astype(jnp.bfloat16)
     placed_coefs = times_rows(coef_bf, order).astype(jnp.bfloat16)
-    orders = (("x", "y", "z"), ("z", "x", "y"))
-    coefs = gather(placed_coefs, row_count, col_count, orders, True, 3)
+    coef_orders = (("x", "y", "z"), ("z", "x", "y"), ("z", "y", "x"))
+    coefs = gather(placed_coefs, row_count, col_count, coef_orders, (2, 3, 3), True, 3)
     result = volume(coefs, centres, nodes)
     back = lax.dot_general(
         split_three(result.T), node_order, (((1,), (0,)), ((), ())), preferred_element_type=jnp.float32

time: 338 us -> 254 us (0.75)
  Pallas kernels: 226 us -> 146 us
  other arithmetic: 30.5 us -> 26.9 us
    pallas_call x1, Pallas kernels: 155 us -> 87 us  [volume(): pl.pallas_call(functools.partial(volume_kernel, groups), out_shape=jax.Sh...]
    pallas_call x3, Pallas kernels: 68.9 us -> 56.7 us  [gather(): pl.pallas_call(functools.partial(gather_kernel, sizes, plans, pair_up), o...]
  transfers between devices with their start and end apart: 1 -> 1, of which waited for: 0 -> 0; matrix products, arithmetic and copies ran while one was open for 11% -> 13% of each run, Pallas kernels for 7% -> 7%
where the time goes in v3:
time: 254 us; the launch traced here: 249 us
  Pallas kernels  146 us (57%)
  matrix products  42.3 us (17%)
  other arithmetic  26.9 us (11%)
  blocking collectives  20.1 us (8%)
  local copies, waits for them, and re-layouts  6.83 us (3%)
  starting transfers between devices  6.35 us (2%)
    pallas_call x1, Pallas kernels, volume(): pl.pallas_call(functools.partial(volume_kernel, groups), out_shape=jax.Sh...  87 us
    pallas_call x3, Pallas kernels, gather(): pl.pallas_call(functools.partial(gather_kernel, sizes, plans, pair_up), o...  56.7 us
    dot_general x6, matrix products, times_rows(): lax.dot_general(left, right, (((1,), (1,)), ((), ())), preferred_element_...  37.1 us
    psum x1, blocking collectives, per_device(): coef_bf = lax.psum(partial_value, 'col').astype(jnp.bfloat16)  20.1 us
    reduce_sum x2, other arithmetic, ranks(): return jnp.sum((key[:, None] < key[None, :]).astype(jnp.int32), axis=0)  10.2 us
    all_to_all x1, starting transfers between devices, per_device(): lax.all_to_all(sent, ('row', 'col'), split_axis=0, concat_axis=0, tiled=T...  6.35 us
  transfers between devices with their start and end apart: 1, of which 0 were waited for; matrix products, arithmetic and copies ran while one was open for 13% of the time, Pallas kernels for 7%

profile of v3, /device:TPU:13, one launch (start us, length us, event | category | flops | bytes accessed | tf_op | source)
XLA Modules:
  0.0 249.1 jit_solution(4918015024918951135)
XLA Ops:
  0.0 0.7 fusion.79
  0.7 0.7 convert_add_fusion
  1.4 0.1 convert_reduce_fusion.2
  1.5 0.7 multiply_add_fusion
  2.2 0.8 reduce-precision_convert_fusion.7
  3.0 0.3 fusion.24
  3.3 0.1 copy.44
  3.5 0.9 reshape.263
  4.4 6.4 %all-to-all-start = ((f32[32,1,784]{2,1,0:T(1,128)}), f32[32,1,784]{2,1,0:T(1,128)}, u32[]{:S(2)}, u32[]{:S(2)}) async-start(f32[32,1,784]{2,1,0:T(1,128)} %reshape.263), calls=%async_computation | async-start | bytes 229376 | tf_op jit(solution)/shard_map/all_to_all | solution.py:344
  10.8 0.9 fusion.93
  11.7 0.8 reduce-precision_convert_fusion.9
  12.5 0.1 fusion.90
  12.6 0.9 reduce-precision_convert_fusion.5
  13.5 0.1 fusion.87
  13.7 1.2 iota_add_fusion
  15.0 8.5 %convert_reduce_fusion = s32[4096]{0:T(1024)S(1)} fusion(s32[4096]{0:T(1024)S(1)} %bitcast.78, s32[4096]{0:T(1024)S(1)} %fusion.59), kind=kLoop, calls=%fused_computation | loop fusion | flops 50327552 | bytes 49152 | tf_op jit(solution)/shard_map/reduce_sum | solution.py:58
  23.5 0.0 copy-start.5
  23.5 2.7 %fusion.2 = f32[9,1024]{1,0:T(8,128)S(1)} fusion(s32[4096]{0:T(1024)S(1)} %convert_reduce_fusion, s32[1024]{0:T(1024)S(1)} %iota_add_fusion.2, bf16[3,4096]{1,0:T(4,128)(2,1)S(1)} %get-tuple-element.31, bf16[3,4096]{1,0:T(4,128)(2,1)S(1)} %get-tuple-element.34, bf16[3,4096]{1,0:T(4,128)(2,1)S(1)} %get-tuple-element.30), kind=kOutput, calls=%fused_computation.3 | convolution fusion | flops 79912960 | bytes 131072 | tf_op jit(solution)/shard_map/dot_general | solution.py:67
  26.2 0.0 copy-done.5
  26.3 13.8 %gather.3 = f32[4,2,2,2,24,128]{5,4,3,2,1,0:T(8,128)S(1)} custom-call(f32[24,128]{1,0:T(8,128)S(1)} %reshape.252.block), custom_call_target="tpu_custom_call" | custom-call | tf_op jit(solution)/shard_map/gather/pallas_call | solution.py:170
  40.1 0.2 reshape_reshape.6
  40.2 0.0 copy-start
  40.3 0.2 copy.38
  40.5 0.0 copy-done.2
  40.5 0.1 iota_add_fusion.1
  40.7 1.7 convert_reduce_fusion.1
  42.4 0.0 copy-start.3
  42.4 3.0 %fusion.5 = f32[9,2048]{0,1:T(8,128)S(1)} fusion(s32[2048]{0:T(1024)S(1)} %convert_reduce_fusion.1, bf16[3,2048]{1,0:T(4,128)(2,1)S(1)} %get-tuple-element.48, bf16[3,2048]{1,0:T(4,128)(2,1)S(1)} %get-tuple-element.50, bf16[3,2048]{1,0:T(4,128)(2,1)S(1)} %get-tuple-element.46), kind=kOutput, calls=%fused_computation.8 | convolution fusion | flops 79802368 | bytes 118784 | tf_op jit(solution)/shard_map/dot_general | solution.py:67
  45.4 1.6 multiply_bitcast_fusion
  47.0 0.0 copy-done
  47.0 0.0 copy-done.3
  47.0 0.6 bitcast_reduce_fusion.2
  47.6 0.1 copy.42
  47.7 0.1 copy.43
  47.8 1.1 reshape_reshape.7
  48.9 1.7 fusion.86
  50.6 2.3 multiply_reduce_fusion
  52.9 0.5 bitcast_reduce_fusion
  53.5 0.1 convert_reduce_fusion.3
  53.6 0.9 fusion.13.place_ref
  54.5 2.6 %compact.1 = s32[256,256]{1,0:T(8,128)} custom-call(s32[256,256]{1,0:T(8,128)} %fusion.13.place_ref), custom_call_target="tpu_custom_call" | custom-call | tf_op jit(solution)/shard_map/compact/pallas_call | solution.py:288
  57.1 1.3 concatenate.28.nodes
  58.4 1.0 pad.5.lists
  59.4 0.0 copy-done.1
  59.4 0.2 broadcast_multiply_fusion
  59.6 0.0 all-to-all-done
  59.6 0.5 broadcast.343
  60.1 1.8 reduce.10
  61.9 0.2 reshape.264
  62.1 0.2 fusion.27
  62.4 0.1 copy.48
  62.5 0.6 fusion.12
  63.1 18.3 %gather.4 = bf16[4,2,48,1024]{3,2,1,0:T(8,128)(2,1)S(1)} custom-call(bf16[48,1024]{1,0:T(8,128)(2,1)S(1)} %fusion.30.block), custom_call_target="tpu_custom_call" | custom-call | tf_op jit(solution)/shard_map/gather/pallas_call | solution.py:170
  81.4 0.1 copy.49
  81.5 0.0 copy-start.6
  81.5 27.6 %fusion.95 = f32[48,4096]{1,0:T(8,128)} fusion(bf16[48,8192]{1,0:T(8,128)(2,1)S(1)} %bitcast.62, bf16[4096,8192]{1,0:T(8,128)(2,1)} %param.7), kind=kOutput, calls=%fused_computation.191 | convolution fusion | flops 3221225472 | bytes 68681728 | tf_op jit(solution)/shard_map/dot_general | solution.py:67
  109.1 20.1 %all-reduce.3 = bf16[48,4096]{1,0:T(8,128)(2,1)S(1)} all-reduce(f32[48,4096]{1,0:T(8,128)} %fusion.95), channel_id=1, replica_groups=mesh['row'=8,'col'=4] {'col'}, use_global_device_ids=true, to_apply=%region_10.11 | all-reduce | flops 196608 | bytes 1179648 | tf_op jit(solution)/shard_map/psum | solution.py:364
  129.2 3.0 %fusion.14.block = bf16[48,1024]{1,0:T(8,128)(2,1)S(1)} fusion(s32[4096]{0:T(1024)S(1)} %copy-done.6, s32[1024]{0:T(1024)S(1)} %iota_add_fusion.2, bf16[48,4096]{1,0:T(8,128)(2,1)S(1)} %all-reduce.3), kind=kOutput, calls=%fused_computation.25 | convolution fusion | flops 406896640 | bytes 512000 | tf_op jit(solution)/shard_map/dot_general | solution.py:67
  132.2 24.5 %gather.5 = bf16[4,2,2,2,48,1024]{5,4,3,2,1,0:T(8,128)(2,1)S(1)} custom-call(bf16[48,1024]{1,0:T(8,128)(2,1)S(1)} %fusion.14.block), custom_call_target="tpu_custom_call" | custom-call | tf_op jit(solution)/shard_map/gather/pallas_call | solution.py:170
  156.8 87.0 %volume.1 = f32[2056,48]{1,0:T(8,128)S(1)} custom-call(s32[256]{0:T(256)S(1)} %get-tuple-element.11.counts, s32[257,264]{1,0:T(8,128)S(1)} %pad.5.lists, f32[3,32768]{1,0:T(4,128)S(1)} %bitcast.60, f32[2056,3]{1,0:T(8,128)S(1)} %concatenate.28.nodes, bf16[32,48,1024]{2,1,0:T(8,128)(2,1)S(1)} %bitcast.58), custom_call_target="tpu_custom_call" | custom-call | tf_op jit(solution)/shard_map/volume/pallas_call | solution.py:306
  243.7 0.3 reduce-precision_convert_fusion.1
  244.0 0.0 copy-done.4
  244.0 4.3 %fusion.4 = f32[144,2048]{1,0:T(8,128)S(1)} fusion(s32[2048]{0:T(1024)S(1)} %copy-done.4, bf16[48,2048]{0,1:T(8,128)(2,1)S(1)} %get-tuple-element.28, bf16[48,2048]{0,1:T(8,128)(2,1)S(1)} %get-tuple-element.29, bf16[48,2048]{0,1:T(8,128)(2,1)S(1)} %get-tuple-element.27), kind=kOutput, calls=%fused_computation.7 | convolution fusion | flops 1213923328 | bytes 1777664 | tf_op jit(solution)/shard_map/dot_general | solution.py:369
  248.3 0.8 slice_add_fusion.2
  (14 shorter events, 0.2 us)
Async XLA Ops:
  0.0 40.5 %copy-start.2 = (f32[3,2048]{1,0:T(4,128)S(1)}, f32[3,2048]{1,0:T(4,128)}, u32[]{:S(2)}) copy-start(f32[3,2048]{1,0:T(4,128)} %param.9) | copy-start | bytes 73732
  4.4 55.2 %all-to-all-start = ((f32[32,1,784]{2,1,0:T(1,128)}), f32[32,1,784]{2,1,0:T(1,128)}, u32[]{:S(2)}, u32[]{:S(2)}) async-start(f32[32,1,784]{2,1,0:T(1,128)} %reshape.263), calls=%async_computation | async-start | bytes 229376 | tf_op jit(solution)/shard_map/all_to_all | solution.py:344
  23.5 2.7 %copy-start.5 = (s32[4096]{0:T(1024)}, s32[4096]{0:T(1024)S(1)}, u32[]{:S(2)}) copy-start(s32[4096]{0:T(1024)S(1)} %convert_reduce_fusion) | copy-start | bytes 49156
  40.2 6.8 %copy-start = (f32[32,3,1024]{2,1,0:T(4,128)}, f32[32,3,1024]{2,1,0:T(4,128)S(1)}, u32[]{:S(2)}) copy-start(f32[32,3,1024]{2,1,0:T(4,128)S(1)} %reshape_reshape.6) | copy-start | bytes 1179652
  42.4 4.6 %copy-start.3 = (s32[2048]{0:T(1024)}, s32[2048]{0:T(1024)S(1)}, u32[]{:S(2)}) copy-start(s32[2048]{0:T(1024)S(1)} %convert_reduce_fusion.1) | copy-start | bytes 24580
  50.6 8.8 %copy-start.1 = (f32[32,3,1024]{2,1,0:T(4,128)S(1)}, f32[32,3,1024]{2,1,0:T(4,128)}, u32[]{:S(2)}) copy-start(f32[32,3,1024]{2,1,0:T(4,128)} %copy-done) | copy-start | bytes 1179652
  81.5 47.7 %copy-start.6 = (s32[4096]{0:T(1024)S(1)}, s32[4096]{0:T(1024)}, u32[]{:S(2)}) copy-start(s32[4096]{0:T(1024)} %copy-done.5) | copy-start | bytes 49156
  132.2 111.8 %copy-start.4 = (s32[2048]{0:T(1024)S(1)}, s32[2048]{0:T(1024)}, u32[]{:S(2)}) copy-start(s32[2048]{0:T(1024)} %copy-done.3) | copy-start | bytes 24580
